TPU v7x, 512 devices: a whole 4x8x8 slice. The times are simulated.
512 devices in a mesh: store: 32 (over x, y), seq: 16 (over z, core).
Axes of the slice: x: 4, y: 8, z: 8, core: 2. Of those that a mesh axis runs over, the one named last changes fastest.
Arguments:
- store_pages: bfloat16 [128, 64, 2048], P('store'), may hold values from -6 to 6
- page_home: int32 [128], replicated, may hold values from 0 to 127, as said below
- doc_page: int32 [32, 3, 8], replicated, may hold values from 0 to 127, as said below
- prefix_len: int32 [32, 3], replicated, may hold values from 1 to 512, as said below
- suffix_q: bfloat16 [32, 1024, 12288], P('store', 'seq'), may hold values from -140 to 140
- suffix_kv: bfloat16 [32, 1024, 2048], P('store', 'seq'), may hold values from -6 to 6
- draft_x: bfloat16 [192, 12288], P(None, 'store'), may hold values from -24 to 24
- w_query: bfloat16 [12288, 12288], P('store', 'seq'), may hold values from -0.0546875 to 0.0546875
- w_keyval: bfloat16 [12288, 2048], P('store'), may hold values from -0.0546875 to 0.0546875
Outputs:
- prefill_out: bfloat16 [32, 1024, 12288], P('store', None, 'seq')
- decode_out: bfloat16 [192, 12288], P('store', 'seq')
Inputs may be any that keep to these rules, and one draw needn't show every extreme that they name: `page_home`: A permutation; slots s * 4 to s * 4 + 3 are held by store device s. `doc_page`: of the 24 entries of one group, at most 2 name pages held by one store device, and in every group some store device holds exactly 2 of them. Entries may repeat. `prefix_len`: some request has the full 512.
All inputs are finite; a program needn't handle non-finite values.
Results may differ from a plain program's by a relative error of at most 0.012.
The roundings to bfloat16 on the way count: a program that leaves them out, or rounds other values in their place, can miss the bound.
Values may be sent and summed in bfloat16 or wider, within the bound.
No kernel may reach another device: no remote copies, remote signals or barrier semaphores. Data moves between devices by JAX's collectives and lax.ppermute only.
A program may use at most 64 MiB of HBM per device.

v0:
```python
import jax
import jax.numpy as jnp
from jax import lax
from jax.sharding import PartitionSpec as P

QH = 96
KVH = 8
HD = 128


def attend(queries, far_keys, far_values, near_keys, near_values, live_mask, causal, score_scale):
    far_scores = jnp.dot(queries, far_keys.T, preferred_element_type=jnp.float32) * score_scale
    near_scores = jnp.dot(queries, near_keys.T, preferred_element_type=jnp.float32) * score_scale
    far_scores = jnp.where(live_mask, far_scores, -1e30)
    near_scores = jnp.where(causal, near_scores, -1e30)
    row_max = jnp.maximum(jnp.max(far_scores, axis=1), jnp.max(near_scores, axis=1))[:, None]
    far_weights = jnp.where(live_mask, jnp.exp(far_scores - row_max), 0.0)
    near_weights = jnp.where(causal, jnp.exp(near_scores - row_max), 0.0)
    row_total = jnp.sum(far_weights, axis=1) + jnp.sum(near_weights, axis=1)
    blended = jnp.dot(
        far_weights.astype(jnp.bfloat16), far_values, preferred_element_type=jnp.float32
    )
    blended = blended + jnp.dot(
        near_weights.astype(jnp.bfloat16), near_values, preferred_element_type=jnp.float32
    )
    return (blended / row_total[:, None]).astype(jnp.bfloat16)


def draft_attention(queries, prefix, drafts, lengths, score_scale):
    half_width = queries.shape[-1]
    far_scores = (
        jnp.einsum(
            "rtvhd,rpvd->rvthp",
            queries,
            prefix[..., :half_width],
            preferred_element_type=jnp.float32,
        )
        * score_scale
    )
    near_scores = (
        jnp.einsum(
            "rtvhd,rsvd->rvths",
            queries,
            drafts[..., :half_width],
            preferred_element_type=jnp.float32,
        )
        * score_scale
    )
    live_mask = (jnp.arange(prefix.shape[1])[None, :] < lengths[:, None])[:, None, None, None, :]
    draft_steps = drafts.shape[1]
    causal = (jnp.arange(draft_steps)[None, :] <= jnp.arange(draft_steps)[:, None])[
        None, None, :, None, :
    ]
    far_scores = jnp.where(live_mask, far_scores, -1e30)
    near_scores = jnp.where(causal, near_scores, -1e30)
    row_max = jnp.maximum(jnp.max(far_scores, axis=4), jnp.max(near_scores, axis=4))[..., None]
    far_weights = jnp.where(live_mask, jnp.exp(far_scores - row_max), 0.0)
    near_weights = jnp.where(causal, jnp.exp(near_scores - row_max), 0.0)
    blended = jnp.einsum(
        "rvthp,rpvd->rtvhd",
        far_weights.astype(jnp.bfloat16),
        prefix[..., half_width:],
        preferred_element_type=jnp.float32,
    )
    blended = blended + jnp.einsum(
        "rvths,rsvd->rtvhd",
        near_weights.astype(jnp.bfloat16),
        drafts[..., half_width:],
        preferred_element_type=jnp.float32,
    )
    row_total = jnp.transpose(
        jnp.sum(far_weights, axis=4) + jnp.sum(near_weights, axis=4), (0, 2, 1, 3)
    )
    return (blended / row_total[..., None]).astype(jnp.bfloat16)


def local(
    store_pages, page_home, doc_page, prefix_len, suffix_q, suffix_kv, draft_x, w_query, w_keyval
):
    store_count = lax.axis_size("store")
    seq_count = lax.axis_size("seq")
    store_index = lax.axis_index("store")
    member = lax.axis_index("seq")
    slot_count = store_pages.shape[0]
    share_count = QH // KVH
    heads_dev = QH // seq_count
    kv_dev = max(1, heads_dev // share_count)
    per_kv = min(heads_dev, share_count)
    width_kv = kv_dev * 2 * HD
    first_kv = member * heads_dev // share_count
    request_count = doc_page.shape[1]
    prefix_span = doc_page.shape[2] * store_pages.shape[1]
    own_pages = lax.dynamic_slice_in_dim(store_pages, first_kv * 2 * HD, width_kv, 2)
    physical = page_home[doc_page.reshape(store_count, -1)]
    need_count = physical.shape[1]
    own_physical = lax.dynamic_index_in_dim(physical, store_index, 0, keepdims=False)
    capacity = max(2, (3 * need_count + 2 * store_count - 1) // (2 * store_count))
    holders = physical // slot_count
    local_slot = physical % slot_count
    wanted = (holders == store_index).astype(jnp.int32)
    holder_rank = jnp.cumsum(wanted, axis=1) - 1
    slot_hits = (wanted[:, None, :] == 1) & (
        holder_rank[:, None, :] == jnp.arange(capacity)[None, :, None]
    )
    slot_pick = jnp.sum(jnp.where(slot_hits, local_slot[:, None, :], 0), axis=2)
    filled = jnp.any(slot_hits, axis=2)
    outgoing = jnp.where(
        filled[:, :, None, None], own_pages[slot_pick], jnp.zeros((), own_pages.dtype)
    )
    incoming = lax.all_to_all(outgoing, "store", split_axis=0, concat_axis=0, tiled=True)
    own_holder = own_physical // slot_count
    matches = (own_holder[:, None] == jnp.arange(store_count)[None, :]).astype(jnp.int32)
    own_rank = jnp.sum(jnp.cumsum(matches, axis=0) * matches, axis=1) - 1
    fetched = incoming.reshape(store_count * capacity, store_pages.shape[1], width_kv)[
        own_holder * capacity + own_rank
    ]
    fetched = fetched.reshape(request_count, prefix_span, kv_dev, 2 * HD)
    local_rows = suffix_q.shape[1]
    query_parts = suffix_q.reshape(local_rows, seq_count, heads_dev * HD)
    kv_heads = (
        jnp.arange(seq_count)[:, None] * heads_dev // share_count + jnp.arange(kv_dev)[None, :]
    ).reshape(-1)
    pair_parts = suffix_kv.reshape(local_rows, KVH, 2 * HD)[:, kv_heads, :]
    head_queries, head_pairs = (
        lax.all_to_all(query_parts, "seq", split_axis=1, concat_axis=0, tiled=True),
        lax.all_to_all(pair_parts, "seq", split_axis=1, concat_axis=0, tiled=True),
    )
    suffix_rows = head_queries.shape[0]
    head_queries = head_queries.reshape(suffix_rows, heads_dev, HD)
    score_scale = HD ** (-0.5)
    lengths = lax.dynamic_index_in_dim(prefix_len, store_index, 0, keepdims=False)
    live_mask = jnp.arange(prefix_span)[None, :] < lengths[0]
    causal = jnp.arange(suffix_rows)[None, :] <= jnp.arange(suffix_rows)[:, None]
    leading = fetched[0]

    def one_head(head_index):
        kv_index = head_index // per_kv
        far_pairs = lax.dynamic_index_in_dim(leading, kv_index, 1, keepdims=False)
        near_pairs = lax.dynamic_index_in_dim(head_pairs, kv_index, 1, keepdims=False)
        query_rows = lax.dynamic_index_in_dim(head_queries, head_index, 1, keepdims=False)
        return attend(
            query_rows,
            far_pairs[:, :HD],
            far_pairs[:, HD:],
            near_pairs[:, :HD],
            near_pairs[:, HD:],
            live_mask,
            causal,
            score_scale,
        )

    head_outputs = lax.map(one_head, jnp.arange(heads_dev, dtype=jnp.int32))
    prefill_out = jnp.transpose(head_outputs, (1, 0, 2)).reshape(1, suffix_rows, heads_dev * HD)
    group_rows = draft_x.shape[0] // store_count
    own_keyval = lax.dynamic_slice_in_dim(w_keyval, first_kv * 2 * HD, width_kv, 1)
    query_term = jnp.dot(draft_x, w_query, preferred_element_type=jnp.float32)
    pair_term = jnp.dot(draft_x, own_keyval, preferred_element_type=jnp.float32)
    summed = lax.psum(jnp.concatenate([query_term, pair_term], axis=1), "store")
    summed = lax.dynamic_slice_in_dim(summed, store_index * group_rows, group_rows, 0)
    query_width = heads_dev * HD
    draft_query = summed[:, :query_width].astype(jnp.bfloat16)
    draft_pairs = summed[:, query_width:].astype(jnp.bfloat16)
    requests = request_count - 1
    draft_steps = group_rows // requests
    decoded = draft_attention(
        draft_query.reshape(requests, draft_steps, kv_dev, per_kv, HD),
        fetched[1:],
        draft_pairs.reshape(requests, draft_steps, kv_dev, 2 * HD),
        lengths[1:],
        score_scale,
    )
    return (prefill_out, decoded.reshape(group_rows, query_width))


def solution(mesh):
    in_specs = (
        P("store", None, None),
        P(),
        P(),
        P(),
        P("store", "seq", None),
        P("store", "seq", None),
        P(None, "store"),
        P("store", "seq"),
        P("store", None),
    )
    out_specs = (P("store", None, "seq"), P("store", "seq"))
    return jax.shard_map(local, mesh=mesh, in_specs=in_specs, out_specs=out_specs, check_vma=False)
```

profile of v0, /device:TPU:1, one launch (start us, length us, event | category | flops | bytes accessed | tf_op | source)
XLA Modules:
  0.0 345.9 jit_solution(14204754690698626446)
XLA Ops:
  0.6 1.8 copy.50
  2.5 1.6 copy.31
  4.1 12.0 %all-to-all-start = ((bf16[64,16,768]{2,0,1:T(8,128)(2,1)}), bf16[64,16,768]{2,0,1:T(8,128)(2,1)S(1)}, u32[]{:S(2)}, u32[]{:S(2)}) async-start(bf16[64,16,768]{2,0,1:T(8,128)(2,1)} %copy.31), calls=%async_computation | async-start | bytes 3145728 | tf_op jit(solution)/shard_map/all_to_all | solution.py:125
  16.3 4.8 %gather_fusion = s32[768]{0:T(1024)S(1)} fusion(s32[128]{0:T(128)S(1)} %copy-done.1, s32[1024]{0:T(1024)S(1)} %pad_clamp_fusion.3), kind=kCustom, calls=%fused_computation | custom fusion | bytes 9216 | tf_op jit(solution)/shard_map/gather | solution.py:94
  22.0 0.9 constant_dynamic-slice_fusion.1
  22.9 2.0 gather_fusion.1
  25.0 3.1 broadcast_select_fusion
  28.1 26.5 %all-to-all-done = bf16[64,16,768]{2,0,1:T(8,128)(2,1)S(1)} async-done(((bf16[64,16,768]{2,0,1:T(8,128)(2,1)}), bf16[64,16,768]{2,0,1:T(8,128)(2,1)S(1)}, u32[]{:S(2)}, u32[]{:S(2)}) %all-to-all-start) | async-done | bytes 1572896 | tf_op jit(solution)/shard_map/all_to_all | solution.py:125
  54.5 9.8 %all-to-all-start.1 = ((bf16[32,2,64,256]{3,2,1,0:T(8,128)(2,1)}), bf16[32,2,64,256]{3,2,1,0:T(8,128)(2,1)}, u32[]{:S(2)}, u32[]{:S(2)}) async-start(bf16[32,2,64,256]{3,2,1,0:T(8,128)(2,1)} %broadcast_select_fusion), calls=%async_computation.1 | async-start | bytes 4194304 | tf_op jit(solution)/shard_map/all_to_all | solution.py:110
  64.6 1.4 fusion.74
  65.9 1.0 pad_maximum_fusion
  66.9 158.9 %all-reduce.1 = bf16[192,1024]{1,0:T(8,128)(2,1)S(1)} all-reduce(f32[192,1024]{1,0:T(8,128)} %pad_maximum_fusion), channel_id=1, replica_groups=mesh['store'=32,'seq'=16] {'store'}, use_global_device_ids=true, to_apply=%region_11.12 | all-reduce | flops 196608 | bytes 1179648 | tf_op jit(solution)/shard_map/psum | solution.py:158
  226.1 0.8 constant_dynamic-slice_fusion.2
  226.8 0.6 slice.50
  227.4 1.0 copy.51
  228.5 1.4 gather_fusion.3
  230.5 30.9 %all-to-all-start.2 = ((bf16[64,16,256]{2,0,1:T(8,128)(2,1)}), bf16[64,16,256]{2,0,1:T(8,128)(2,1)}, u32[]{:S(2)}, u32[]{:S(2)}) async-start(bf16[64,16,256]{2,0,1:T(8,128)(2,1)} %bitcast.140), calls=%async_computation.2 | async-start | bytes 1048576 | tf_op jit(solution)/shard_map/all_to_all | solution.py:126
  261.4 2.8 reshape.417
  264.2 2.9 copy.41
  267.1 2.2 gather_fusion.2
  270.4 0.6 copy.54
  271.0 7.8 %all-to-all-done.2 = bf16[64,16,256]{2,0,1:T(8,128)(2,1)} async-done(((bf16[64,16,256]{2,0,1:T(8,128)(2,1)}), bf16[64,16,256]{2,0,1:T(8,128)(2,1)}, u32[]{:S(2)}, u32[]{:S(2)}) %all-to-all-start.2) | async-done | bytes 524320 | tf_op jit(solution)/shard_map/all_to_all | solution.py:126
  278.8 64.5 %while.12 = (s32[]{:T(128)}, bf16[6,1024,128]{1,2,0:T(8,128)(2,1)}, s32[6]{0:T(128)S(1)}, bf16[1024,6,128]{2,0,1:T(8,128)(2,1)}, bf16[512,1,256]{2,0,1:T(8,128)(...) while((s32[]{:T(128)}, bf16[6,1024,128]{1,2,0:T(8,128)(2,1)}, ...), condition=%wide.region_10.11_spmd.clone.clone, body=%wide.region_5.10_spmd.clone.clone.sunk | while | flops 829291008 | bytes 22608544 | solution.py:152
  278.8 0.6 dynamic_slice.65
  281.2 0.7 compare_reduce_fusion.2
  281.9 1.4 fusion.95
  283.3 1.7 fusion.94
  286.1 1.7 fusion.96
  287.8 0.9 fusion.99
  288.9 0.7 constant_dynamic-update-slice_fusion.2
  289.6 0.6 dynamic_slice.65
  291.9 0.7 compare_reduce_fusion.2
  292.6 1.4 fusion.95
  294.0 1.7 fusion.94
  296.8 1.7 fusion.96
  298.5 0.9 fusion.99
  299.6 0.7 constant_dynamic-update-slice_fusion.2
  300.3 0.6 dynamic_slice.65
  302.6 0.7 compare_reduce_fusion.2
  303.3 1.4 fusion.95
  304.7 1.7 fusion.94
  307.6 1.7 fusion.96
  309.3 0.9 fusion.99
  310.3 0.7 constant_dynamic-update-slice_fusion.2
  311.0 0.6 dynamic_slice.65
  313.4 0.7 compare_reduce_fusion.2
  314.1 1.4 fusion.95
  315.5 1.8 fusion.94
  318.3 1.7 fusion.96
  320.0 0.9 fusion.99
  321.1 0.7 constant_dynamic-update-slice_fusion.2
  324.1 0.7 compare_reduce_fusion.2
  324.8 1.4 fusion.95
  326.2 1.8 fusion.94
  329.1 1.7 fusion.96
  330.8 0.9 fusion.99
  331.8 0.7 constant_dynamic-update-slice_fusion.2
  334.9 0.7 compare_reduce_fusion.2
  335.6 1.4 fusion.95
  337.0 1.8 fusion.94
  339.8 1.7 fusion.96
  341.5 0.9 fusion.99
  342.6 0.7 constant_dynamic-update-slice_fusion.2
  343.3 2.6 copy.43
  (90 shorter events, 11.6 us)
Async XLA Ops:
  0.6 63.7 %copy-start = (bf16[384,2048]{1,0:T(8,128)(2,1)S(1)}, bf16[384,2048]{1,0:T(8,128)(2,1)}, u32[]{:S(2)}) copy-start(bf16[384,2048]{1,0:T(8,128)(2,1)} %param.19) | copy-start | bytes 4718596
  4.1 12.0 %copy-start.3 = (s32[32,3,8]{0,2,1:T(8,128)S(1)}, s32[32,3,8]{0,2,1:T(8,128)}, u32[]{:S(2)}) copy-start(s32[32,3,8]{0,2,1:T(8,128)} %param.13) | copy-start | bytes 9220
  4.1 12.2 %copy-start.1 = (s32[128]{0:T(128)S(1)}, s32[128]{0:T(128)}, u32[]{:S(2)}) copy-start(s32[128]{0:T(128)} %param.12) | copy-start | bytes 1540
  4.1 50.4 %all-to-all-start = ((bf16[64,16,768]{2,0,1:T(8,128)(2,1)}), bf16[64,16,768]{2,0,1:T(8,128)(2,1)S(1)}, u32[]{:S(2)}, u32[]{:S(2)}) async-start(bf16[64,16,768]{2,0,1:T(8,128)(2,1)} %copy.31), calls=%async_computation | async-start | bytes 3145728 | tf_op jit(solution)/shard_map/all_to_all | solution.py:125
  28.0 36.3 %copy-start.2 = (bf16[192,384]{1,0:T(8,128)(2,1)S(1)}, bf16[192,384]{1,0:T(8,128)(2,1)}, u32[]{:S(2)}) copy-start(bf16[192,384]{1,0:T(8,128)(2,1)} %param.17) | copy-start | bytes 442372
  54.5 176.0 %all-to-all-start.1 = ((bf16[32,2,64,256]{3,2,1,0:T(8,128)(2,1)}), bf16[32,2,64,256]{3,2,1,0:T(8,128)(2,1)}, u32[]{:S(2)}, u32[]{:S(2)}) async-start(bf16[32,2,64,256]{3,2,1,0:T(8,128)(2,1)} %broadcast_select_fusion), calls=%async_computation.1 | async-start | bytes 4194304 | tf_op jit(solution)/shard_map/all_to_all | solution.py:110
  230.5 48.4 %all-to-all-start.2 = ((bf16[64,16,256]{2,0,1:T(8,128)(2,1)}), bf16[64,16,256]{2,0,1:T(8,128)(2,1)}, u32[]{:S(2)}, u32[]{:S(2)}) async-start(bf16[64,16,256]{2,0,1:T(8,128)(2,1)} %bitcast.140), calls=%async_computation.2 | async-start | bytes 1048576 | tf_op jit(solution)/shard_map/all_to_all | solution.py:126
where the time goes:
time: 347 us; the launch traced here: 346 us
  blocking collectives  159 us (46%)
  starting transfers between devices  52.7 us (15%)
  matrix products  36.9 us (11%)
  local copies, waits for them, and re-layouts  35.9 us (10%)
  waiting for transfers between devices  34.3 us (10%)
  other arithmetic  15.7 us (5%)
  loops' own time  10.7 us (3%)
    psum x1, blocking collectives, local(): summed = lax.psum(jnp.concatenate([query_term, pair_term], axis=1), 'store')  159 us
    all_to_all x1, starting transfers between devices, local(): lax.all_to_all(pair_parts, 'seq', split_axis=1, concat_axis=0, tiled=True)  30.9 us
    all_to_all x1, waiting for transfers between devices, local(): lax.all_to_all(query_parts, 'seq', split_axis=1, concat_axis=0, tiled=True)  26.5 us
    all_to_all x1, starting transfers between devices, local(): lax.all_to_all(query_parts, 'seq', split_axis=1, concat_axis=0, tiled=True)  12 us
    another operation x1, loops' own time, local(): head_outputs = lax.map(one_head, jnp.arange(heads_dev, dtype=jnp.int32))  10.7 us
    dot_general x6, matrix products, attend(): jnp.dot(queries, near_keys.T, preferred_element_type=jnp.float32)  10.5 us
    dot_general x6, matrix products, attend(): jnp.dot(near_weights.astype(jnp.bfloat16), near_values, preferred_element...  10.2 us
    all_to_all x1, starting transfers between devices, local(): lax.all_to_all(outgoing, 'store', split_axis=0, concat_axis=0, tiled=True)  9.8 us
  transfers between devices with their start and end apart: 3, of which 2 were waited for; matrix products, arithmetic and copies ran while one was open for 8% of the time, Pallas kernels for 0%

commit v1 on v0

v1 whole, which is shorter than its diff:
```python
import functools

import jax
import jax.numpy as jnp
from jax import lax
from jax.experimental import pallas as pl
from jax.experimental.pallas import tpu as pltpu
from jax.sharding import PartitionSpec as P

QH = 96
KVH = 8
HD = 128
X = 4
Y = 8
SEQ = 16
HEADS = 6
PAGE = 64
SLOTS = 4
NEED = 24
PREF = 512
SUF = 1024
ROWS = SUF // SEQ
DEC = 6
COLS = HEADS * HD + HD
BLOCKS = COLS // HD
PAGE_ROWS = SLOTS * PAGE
PART = X * DEC
SEND_Y = PAGE_ROWS + BLOCKS * 2 * PART
PICKS = 2 * Y
SEND_X = PICKS * PAGE + BLOCKS * 16
FETCH = NEED * PAGE
SWAP = FETCH + 16
SCALE = HD ** (-0.5)
EXP2 = SCALE * 1.4426950408889634
F32 = jnp.float32
BF16 = jnp.bfloat16
SMEM = pl.BlockSpec(memory_space=pltpu.SMEM)
VMEM = pl.BlockSpec(memory_space=pltpu.VMEM)


def params(mib):
    return pltpu.CompilerParams(vmem_limit_bytes=mib * 1024 * 1024)


def dot(a, b):
    return jnp.dot(a, b, preferred_element_type=F32)


def dot_t(a, b):
    return lax.dot_general(a, b, (((1,), (1,)), ((), ())), preferred_element_type=F32)


def split(values):
    high = values.astype(BF16).astype(F32)
    return jnp.concatenate([high, values - high], axis=0).astype(BF16)


def pack_kernel(q_ref, kv_ref, out_ref):
    out_ref[0, :, : HEADS * HD] = q_ref[...]
    out_ref[0, :, HEADS * HD :] = kv_ref[...]


def pack(queries, pairs):
    return pl.pallas_call(
        pack_kernel,
        grid=(SEQ,),
        in_specs=[
            pl.BlockSpec((ROWS, HEADS * HD), lambda i: (0, i)),
            pl.BlockSpec((ROWS, HD), lambda i: (0, i)),
        ],
        out_specs=pl.BlockSpec((1, ROWS, COLS), lambda i: (i, 0, 0)),
        out_shape=jax.ShapeDtypeStruct((SEQ, ROWS, COLS), BF16),
        compiler_params=params(16),
    )(queries, pairs)


def project_kernel(place, x_ref, wq_ref, wkv_ref, pages_ref, *outs):
    my_y = place[1]
    rows = Y * PART
    row = lax.broadcasted_iota(jnp.int32, (rows, rows), 0)
    col = lax.broadcasted_iota(jnp.int32, (rows, rows), 1)
    step, inner = row // PART, row % PART
    to_x, item = inner // DEC, inner % DEC
    to_y = (my_y + step) % Y
    pick = (col == (to_x * Y + to_y) * DEC + item).astype(F32).astype(BF16)
    ordered = dot(pick, x_ref[...]).astype(BF16)
    terms = [dot(ordered, wq_ref[...]), dot(ordered, wkv_ref[...])]
    pages = pages_ref[...].reshape(PAGE_ROWS, HD)
    for k in range(Y):
        outs[k][:PAGE_ROWS, :] = pages
        for n in range(BLOCKS):
            term = terms[0][:, n * HD : (n + 1) * HD] if n < HEADS else terms[1]
            base = PAGE_ROWS + n * 2 * PART
            outs[k][base : base + 2 * PART, :] = split(term[k * PART : (k + 1) * PART])


def project(place, x, w_query, w_keyval, store_pages):
    width = x.shape[1]
    return pl.pallas_call(
        project_kernel,
        grid_spec=pltpu.PrefetchScalarGridSpec(
            num_scalar_prefetch=1,
            grid=(1,),
            in_specs=[
                pl.BlockSpec((Y * PART, width), lambda i, p: (0, 0)),
                pl.BlockSpec((width, HEADS * HD), lambda i, p: (0, 0)),
                pl.BlockSpec((width, HD), lambda i, p: (0, p[2])),
                pl.BlockSpec((SLOTS, PAGE, HD), lambda i, p: (0, 0, p[2])),
            ],
            out_specs=[pl.BlockSpec((SEND_Y, HD), lambda i, p: (0, 0))] * Y,
        ),
        out_shape=[jax.ShapeDtypeStruct((SEND_Y, HD), BF16)] * Y,
        compiler_params=params(24),
    )(place, x, w_query, w_keyval, store_pages)


def route_kernel(place, doc, home, *refs):
    got, outs = refs[:Y], refs[Y : Y + X]
    pages, picks, seen = refs[Y + X :]
    my_x, my_y = place[0], place[1]
    for k in range(Y):
        pages[k * PAGE_ROWS : (k + 1) * PAGE_ROWS, :] = got[k][:PAGE_ROWS, :]

    def clear(i, carry):
        picks[i] = 0
        seen[2 * i] = 0
        seen[2 * i + 1] = 0
        return carry

    lax.fori_loop(0, X * PICKS, clear, 0)

    def note(i, carry):
        k = i // NEED
        group = ((my_x + k) % X) * Y + my_y
        place_in = home[doc[group * NEED + i - k * NEED]]
        holder = place_in // SLOTS
        rank = seen[k * X * Y + holder]
        seen[k * X * Y + holder] = rank + 1
        holder_y = holder % Y

        @pl.when(holder // Y == my_x)
        def _():
            spot = k * PICKS + holder_y * 2 + jnp.minimum(rank, 1)
            picks[spot] = ((my_y + Y - holder_y) % Y) * SLOTS + place_in % SLOTS

        return carry

    lax.fori_loop(0, X * NEED, note, 0)
    for k in range(X):
        for i in range(PICKS):
            start = pl.multiple_of(picks[k * PICKS + i] * PAGE, PAGE)
            outs[k][i * PAGE : (i + 1) * PAGE, :] = pages[pl.ds(start, PAGE), :]
    row = lax.broadcasted_iota(jnp.int32, (16, 2 * PART), 0)
    col = lax.broadcasted_iota(jnp.int32, (16, 2 * PART), 1)
    wanted = [
        (
            (row % 8 < DEC) & (col == (row // 8) * PART + ((my_x + k) % X) * DEC + row % 8)
        ).astype(F32).astype(BF16)
        for k in range(X)
    ]
    for n in range(BLOCKS):
        base = PAGE_ROWS + n * 2 * PART
        total = jnp.zeros((2 * PART, HD), F32)
        for k in range(Y):
            total = total + got[k][base : base + 2 * PART, :].astype(F32)
        both = split(total[:PART] + total[PART:])
        for k in range(X):
            spot = PICKS * PAGE + n * 16
            outs[k][spot : spot + 16, :] = dot(wanted[k], both).astype(BF16)


def route(place, doc, home, got):
    return pl.pallas_call(
        route_kernel,
        in_specs=[SMEM] * 3 + [VMEM] * Y,
        out_specs=[VMEM] * X,
        out_shape=[jax.ShapeDtypeStruct((SEND_X, HD), BF16)] * X,
        scratch_shapes=[
            pltpu.VMEM((Y * PAGE_ROWS, HD), BF16),
            pltpu.SMEM((X * PICKS,), jnp.int32),
            pltpu.SMEM((X * X * Y,), jnp.int32),
        ],
        compiler_params=params(16),
    )(place, doc, home, *got)


def collect_kernel(place, doc, home, *refs):
    got, (out_ref, q_ref), (seen,) = refs[:X], refs[X : X + 2], refs[X + 2 :]
    my_x, my_y = place[0], place[1]
    group = my_x * Y + my_y

    def clear(i, carry):
        seen[i] = 0
        return carry

    lax.fori_loop(0, X * Y, clear, 0)

    def note(i, carry):
        holder = home[doc[group * NEED + i]] // SLOTS
        rank = seen[holder]
        seen[holder] = rank + 1
        spot = (holder % Y) * 2 + jnp.minimum(rank, 1)
        start = pl.multiple_of(spot * PAGE, PAGE)
        far = (my_x + X - holder // Y) % X
        target = pl.ds(pl.multiple_of(i * PAGE, PAGE), PAGE)
        for k in range(X):

            @pl.when(far == k)
            def _():
                out_ref[target, :] = got[k][pl.ds(start, PAGE), :]

        return carry

    lax.fori_loop(0, NEED, note, 0)
    blank = jnp.zeros((8, HD), F32)
    for n in range(BLOCKS):
        spot = PICKS * PAGE + n * 16
        total = jnp.zeros((16, HD), F32)
        for k in range(X):
            total = total + got[k][spot : spot + 16, :].astype(F32)
        value = jnp.concatenate([total[:8] + total[8:], blank], axis=0).astype(BF16)
        if n < HEADS:
            q_ref[:, n * HD : (n + 1) * HD] = value
        else:
            out_ref[FETCH:, :] = value


def collect(place, doc, home, got):
    return pl.pallas_call(
        collect_kernel,
        in_specs=[SMEM] * 3 + [VMEM] * X,
        out_specs=[VMEM] * 2,
        out_shape=[
            jax.ShapeDtypeStruct((SWAP, HD), BF16),
            jax.ShapeDtypeStruct((16, HEADS * HD), BF16),
        ],
        scratch_shapes=[pltpu.SMEM((X * Y,), jnp.int32)],
        compiler_params=params(16),
    )(place, doc, home, *got)


def decode_kernel(place, lens, mine, other, q_ref, out_ref, keys, values):
    @pl.when(place[3] == 0)
    def _():
        keys[...] = mine[PREF:, :]
        values[...] = other[PREF:, :]

    @pl.when(place[3] == 1)
    def _():
        keys[...] = other[PREF:, :]
        values[...] = mine[PREF:, :]

    rows = HEADS * 8
    queries = jnp.concatenate(
        [q_ref[:, h * HD : (h + 1) * HD].astype(F32)[:8] for h in range(HEADS)], axis=0
    ).astype(BF16)
    half = DEC // 2
    item = lax.broadcasted_iota(jnp.int32, (rows, PREF), 0) % 8
    spot = lax.broadcasted_iota(jnp.int32, (rows, PREF), 1)
    scores, live = [], []
    for d in range(2):
        raw = dot_t(queries, keys[d * PREF : (d + 1) * PREF, :]) * SCALE
        ok = (item // half == d) & (spot < lens[d + 1])
        live.append(ok)
        scores.append(jnp.where(ok, raw, -1e30))
    near = dot_t(queries, keys[2 * PREF :, :]) * SCALE
    row = lax.broadcasted_iota(jnp.int32, near.shape, 0) % 8
    col = lax.broadcasted_iota(jnp.int32, near.shape, 1)
    near_ok = (col <= row) & (col // half == row // half) & (col < DEC)
    near = jnp.where(near_ok, near, -1e30)
    top = jnp.max(near, axis=1, keepdims=True)
    for part in scores:
        top = jnp.maximum(top, jnp.max(part, axis=1, keepdims=True))
    weight = jnp.where(near_ok, jnp.exp(near - top), 0.0)
    total = jnp.sum(weight, axis=1, keepdims=True)
    blend = dot(weight.astype(BF16), values[2 * PREF :, :])
    for d in range(2):
        weight = jnp.where(live[d], jnp.exp(scores[d] - top), 0.0)
        total = total + jnp.sum(weight, axis=1, keepdims=True)
        blend = blend + dot(weight.astype(BF16), values[d * PREF : (d + 1) * PREF, :])
    blend = blend / total
    for h in range(HEADS):
        out_ref[:, h * HD : (h + 1) * HD] = blend[h * 8 : h * 8 + DEC].astype(BF16)


def decode(place, lens, mine, other, queries):
    return pl.pallas_call(
        decode_kernel,
        in_specs=[SMEM] * 2 + [VMEM] * 3,
        out_specs=VMEM,
        out_shape=jax.ShapeDtypeStruct((DEC, HEADS * HD), BF16),
        scratch_shapes=[pltpu.VMEM((SWAP - PREF, HD), BF16)] * 2,
        compiler_params=params(16),
    )(place, lens, mine, other, queries)


TILE = 256


def prefill_kernel(place, lens, far_mine, far_other, near_mine, near_other, q_ref, out_ref, keys, values):
    @pl.when(pl.program_id(0) == 0)
    def _():
        def fill(far_keys, far_values, near_keys, near_values):
            alive = lax.broadcasted_iota(jnp.int32, (PREF, HD), 0) < lens[0]
            held = far_keys[:PREF, :].astype(F32)
            keys[:PREF, :] = jnp.where(alive, held, held[0:1]).astype(BF16)
            keys[PREF:, :] = near_keys[...]
            held = far_values[:PREF, :].astype(F32)
            values[:PREF, :HD] = jnp.where(alive, held, 0.0).astype(BF16)
            values[PREF:, :HD] = near_values[...]
            values[:PREF, HD:] = jnp.where(alive, 1.0, 0.0).astype(BF16)
            values[PREF:, HD:] = jnp.ones((SUF, HD), BF16)

        @pl.when(place[3] == 0)
        def _():
            fill(far_mine, far_other, near_mine, near_other)

        @pl.when(place[3] == 1)
        def _():
            fill(far_other, far_mine, near_other, near_mine)

    row = lax.broadcasted_iota(jnp.int32, (TILE, TILE), 0)
    col = lax.broadcasted_iota(jnp.int32, (TILE, TILE), 1)
    for i in range(SUF // TILE):
        done = PREF + i * TILE
        queries = q_ref[i * TILE : (i + 1) * TILE, :]
        full = dot_t(queries, keys[:done, :])
        edge = dot_t(queries, keys[done : done + TILE, :])
        edge = jnp.where(col <= row, edge, -1e30)
        top = jnp.maximum(
            jnp.max(full, axis=1, keepdims=True), jnp.max(edge, axis=1, keepdims=True)
        )
        blend = dot(jnp.exp2((full - top) * EXP2).astype(BF16), values[:done, :])
        blend = blend + dot(
            jnp.exp2((edge - top) * EXP2).astype(BF16), values[done : done + TILE, :]
        )
        out_ref[i * TILE : (i + 1) * TILE, :] = (blend[:, :HD] / blend[:, HD:]).astype(BF16)


def prefill(place, lens, far_mine, far_other, near_mine, near_other, queries):
    whole = lambda a: pl.BlockSpec(a.shape, lambda h: (0, 0))
    return pl.pallas_call(
        prefill_kernel,
        grid=(HEADS,),
        in_specs=[
            SMEM,
            SMEM,
            pl.BlockSpec((PREF, HD), lambda h: (0, 0)),
            pl.BlockSpec((PREF, HD), lambda h: (0, 0)),
            whole(near_mine),
            whole(near_other),
            pl.BlockSpec((SUF, HD), lambda h: (0, h)),
        ],
        out_specs=pl.BlockSpec((SUF, HD), lambda h: (0, h)),
        out_shape=jax.ShapeDtypeStruct((SUF, HEADS * HD), BF16),
        scratch_shapes=[
            pltpu.VMEM((PREF + SUF, HD), BF16),
            pltpu.VMEM((PREF + SUF, 2 * HD), BF16),
        ],
        compiler_params=params(40),
    )(place, lens, far_mine, far_other, near_mine, near_other, queries)


def local(
    store_pages, page_home, doc_page, prefix_len, suffix_q, suffix_kv, draft_x, w_query, w_keyval
):
    store_index = lax.axis_index("store")
    member = lax.axis_index("seq")
    place = jnp.stack([store_index // Y, store_index % Y, member, member % 2]).astype(jnp.int32)
    lens = lax.dynamic_index_in_dim(prefix_len, store_index, 0, keepdims=False)
    doc = doc_page.reshape(-1)
    along_y = lambda k: [(x * Y + y, x * Y + (y + k) % Y) for x in range(X) for y in range(Y)]
    along_x = lambda k: [(x * Y + y, (x + k) % X * Y + y) for x in range(X) for y in range(Y)]
    twins = [(i, i ^ 1) for i in range(SEQ)]

    packed = pack(suffix_q.reshape(ROWS, -1), suffix_kv.reshape(ROWS, -1))
    turned = lax.all_to_all(packed, "seq", split_axis=0, concat_axis=0, tiled=True)
    turned = turned.reshape(SUF, COLS)

    sent = project(place, draft_x, w_query, w_keyval, store_pages)
    got = [sent[0]] + [lax.ppermute(sent[k], "store", along_y(k)) for k in range(1, Y)]
    sent = route(place, doc, page_home, got)
    got = [sent[0]] + [lax.ppermute(sent[k], "store", along_x(k)) for k in range(1, X)]
    far_mine, draft_query = collect(place, doc, page_home, got)
    far_other = lax.ppermute(far_mine, "seq", twins)
    decoded = decode(place, lens, far_mine, far_other, draft_query)

    near_mine = turned[:, HEADS * HD :]
    near_other = lax.ppermute(near_mine, "seq", twins)
    prefilled = prefill(place, lens, far_mine, far_other, near_mine, near_other, turned)
    return prefilled.reshape(1, SUF, HEADS * HD), decoded


def solution(mesh):
    in_specs = (
        P("store", None, None),
        P(),
        P(),
        P(),
        P("store", "seq", None),
        P("store", "seq", None),
        P(None, "store"),
        P("store", "seq"),
        P("store", None),
    )
    out_specs = (P("store", None, "seq"), P("store", "seq"))
    return jax.shard_map(local, mesh=mesh, in_specs=in_specs, out_specs=out_specs, check_vma=False)
```

time: 347 us -> 121 us (0.35)
  the two profiles are of different devices: /device:TPU:1 before, /device:TPU:11 now
where the time goes in v1:
time: 121 us
  starting transfers between devices  52.6 us (43%)
  waiting for transfers between devices  29.7 us (25%)
  Pallas kernels  28.6 us (24%)
  local copies, waits for them, and re-layouts  8.8 us (7%)
    ppermute x7, starting transfers between devices, local(): lax.ppermute(sent[k], 'store', along_y(k))  27.5 us
    ppermute x7, waiting for transfers between devices, local(): lax.ppermute(sent[k], 'store', along_y(k))  17.8 us
    pallas_call x1, Pallas kernels, prefill(): pl.pallas_call(prefill_kernel, grid=(HEADS,), in_specs=[SMEM, SMEM, pl.Bl...  16.5 us
    ppermute x3, waiting for transfers between devices, local(): lax.ppermute(sent[k], 'store', along_x(k))  11.9 us
    all_to_all x1, starting transfers between devices, local(): lax.all_to_all(packed, 'seq', split_axis=0, concat_axis=0, tiled=True)  11.1 us
    ppermute x3, starting transfers between devices, local(): lax.ppermute(sent[k], 'store', along_x(k))  9.64 us
    unnamed x25, local copies, waits for them, and re-layouts  8.49 us
    pallas_call x1, Pallas kernels, route(): pl.pallas_call(route_kernel, in_specs=[SMEM] * 3 + [VMEM] * Y, out_specs=...  5.75 us
  transfers between devices with their start and end apart: 13, of which 6 were waited for; matrix products, arithmetic and copies ran while one was open for 0% of the time, Pallas kernels for 10%

profile of v1, /device:TPU:11, one launch (start us, length us, event | category | flops | bytes accessed | tf_op | source)
XLA Modules:
  0.0 120.7 jit_solution(8719412455984292168)
XLA Ops:
  0.6 0.0 copy-start
  0.6 0.0 copy-start.2
  0.7 1.4 %copy-done.2 = bf16[1,64,12288]{2,1,0:T(8,128)(2,1)S(1)} copy-done((bf16[1,64,12288]{2,1,0:T(8,128)(2,1)S(1)}, bf16[1,64,12288]{2,1,0:T(8,128)(2,1)}, u32[]{:S(2)}) %copy-start.2) | copy-done | bytes 1572888
  2.1 0.0 copy-start.6
  2.1 0.9 copy-done.6
  3.0 0.7 shard_map.107
  3.7 0.0 copy-start.1
  3.7 1.2 %copy-done.1 = bf16[16,64,896]{2,1,0:T(8,128)(2,1)} copy-done((bf16[16,64,896]{2,1,0:T(8,128)(2,1)}, bf16[16,64,896]{2,1,0:T(8,128)(2,1)S(1)}, u32[]{:S(2)}) %copy-start.1) | copy-done | bytes 1835032
  4.9 0.0 copy-start.3
  4.9 11.1 %all-to-all-start = ((bf16[16,64,896]{2,1,0:T(8,128)(2,1)}), bf16[16,64,896]{2,1,0:T(8,128)(2,1)S(1)}, u32[]{:S(2)}, u32[]{:S(2)}) async-start(bf16[16,64,896]{2,1,0:T(8,128)(2,1)} %copy-done.1), calls=%async_computation | async-start | bytes 3670016 | tf_op jit(solution)/shard_map/all_to_all | solution.py:377
  16.1 0.1 pad_add_fusion.place
  16.2 0.0 copy-done.3
  16.2 0.0 copy-start.4
  16.2 1.2 %copy-done.4 = bf16[4,64,2048]{2,1,0:T(8,128)(2,1)S(1)} copy-done((bf16[4,64,2048]{2,1,0:T(8,128)(2,1)S(1)}, bf16[4,64,2048]{2,1,0:T(8,128)(2,1)}, u32[]{:S(2)}) %copy-start.4) | copy-done | bytes 1048600
  17.4 0.0 copy-start.5
  17.4 1.1 copy-done.5
  18.4 0.0 copy-start.9
  18.4 0.9 copy-done.9
  19.4 0.0 copy-start.11
  19.4 0.0 copy-start.10
  19.4 2.0 %shard_map.104 = (bf16[592,128]{1,0:T(8,128)(2,1)S(1)}, bf16[592,128]{1,0:T(8,128)(2,1)S(1)}, bf16[592,128]{1,0:T(8,128)(2,1)S(1)}, bf16[592,128]{1,0:T(8,128)(2...) custom-call(s32[4]{0:T(128)S(1)} %pad_add_fusion.place, ...), custom_call_target="tpu_custom_call" | custom-call | tf_op jit(solution)/shard_map/pallas_call | solution.py:99
  21.4 0.0 copy-start.7
  21.4 0.7 copy-done.7
  22.0 3.2 %collective-permute-start = (bf16[592,128]{1,0:T(8,128)(2,1)S(1)}, bf16[592,128]{1,0:T(8,128)(2,1)S(1)}, u32[]{:S(2)}, u32[]{:S(2)}) collective-permute-start(bf16[592,128]{1,0:T(8,128)(2,1)S(1)} %get-tuple-element.17), channel_id=1, source_target_pairs={{0,16},{16,32},{32,48},{48,64},{64,80},{80,96},{96,112},{112,0},{1... | collective-permute-start | bytes 454664 | tf_op jit(solution)/shard_map/ppermute | solution.py:381
  25.2 5.4 %collective-permute-start.1 = (bf16[592,128]{1,0:T(8,128)(2,1)S(1)}, bf16[592,128]{1,0:T(8,128)(2,1)S(1)}, u32[]{:S(2)}, u32[]{:S(2)}) collective-permute-start(bf16[592,128]{1,0:T(8,128)(2,1)S(1)} %get-tuple-element.18), channel_id=1, source_target_pairs={{0,32},{16,48},{32,64},{48,80},{64,96},{80,112},{96,0},{112,16},{1... | collective-permute-start | bytes 454664 | tf_op jit(solution)/shard_map/ppermute | solution.py:381
  30.7 2.5 %collective-permute-start.2 = (bf16[592,128]{1,0:T(8,128)(2,1)}, bf16[592,128]{1,0:T(8,128)(2,1)S(1)}, u32[]{:S(2)}, u32[]{:S(2)}) collective-permute-start(bf16[592,128]{1,0:T(8,128)(2,1)} %get-tuple-element.19), channel_id=1, source_target_pairs={{0,48},{16,64},{32,80},{48,96},{64,112},{80,0},{96,16},{112,32},{1... | collective-permute-start | bytes 454664 | tf_op jit(solution)/shard_map/ppermute | solution.py:381
  33.2 4.4 %collective-permute-start.3 = (bf16[592,128]{1,0:T(8,128)(2,1)}, bf16[592,128]{1,0:T(8,128)(2,1)S(1)}, u32[]{:S(2)}, u32[]{:S(2)}) collective-permute-start(bf16[592,128]{1,0:T(8,128)(2,1)} %get-tuple-element.20), channel_id=1, source_target_pairs={{0,64},{16,80},{32,96},{48,112},{64,0},{80,16},{96,32},{112,48},{1... | collective-permute-start | bytes 454664 | tf_op jit(solution)/shard_map/ppermute | solution.py:381
  37.7 3.6 %collective-permute-start.4 = (bf16[592,128]{1,0:T(8,128)(2,1)}, bf16[592,128]{1,0:T(8,128)(2,1)S(1)}, u32[]{:S(2)}, u32[]{:S(2)}) collective-permute-start(bf16[592,128]{1,0:T(8,128)(2,1)} %get-tuple-element.21), channel_id=1, source_target_pairs={{0,80},{16,96},{32,112},{48,0},{64,16},{80,32},{96,48},{112,64},{1... | collective-permute-start | bytes 454664 | tf_op jit(solution)/shard_map/ppermute | solution.py:381
  41.2 0.0 collective-permute-done.refs_1_
  41.3 4.1 %collective-permute-start.5 = (bf16[592,128]{1,0:T(8,128)(2,1)}, bf16[592,128]{1,0:T(8,128)(2,1)S(1)}, u32[]{:S(2)}, u32[]{:S(2)}) collective-permute-start(bf16[592,128]{1,0:T(8,128)(2,1)} %get-tuple-element.22), channel_id=1, source_target_pairs={{0,96},{16,112},{32,0},{48,16},{64,32},{80,48},{96,64},{112,80},{1... | collective-permute-start | bytes 454664 | tf_op jit(solution)/shard_map/ppermute | solution.py:381
  45.4 0.0 collective-permute-done.1.refs_2_
  45.4 4.2 %collective-permute-start.6 = (bf16[592,128]{1,0:T(8,128)(2,1)}, bf16[592,128]{1,0:T(8,128)(2,1)S(1)}, u32[]{:S(2)}, u32[]{:S(2)}) collective-permute-start(bf16[592,128]{1,0:T(8,128)(2,1)} %get-tuple-element.23), channel_id=1, source_target_pairs={{0,112},{16,0},{32,16},{48,32},{64,48},{80,64},{96,80},{112,96},{1... | collective-permute-start | bytes 454664 | tf_op jit(solution)/shard_map/ppermute | solution.py:381
  49.6 0.0 copy-done.11
  49.6 0.1 copy.11
  49.7 0.1 reshape.19.doc
  49.8 0.0 collective-permute-done.2.refs_3_
  49.8 0.0 collective-permute-done.3.refs_4_
  49.8 8.6 %collective-permute-done.4.refs_5_ = bf16[592,128]{1,0:T(8,128)(2,1)S(1)} collective-permute-done((bf16[592,128]{1,0:T(8,128)(2,1)}, bf16[592,128]{1,0:T(8,128)(2,1)S(1)}, u32[]{:S(2)}, u32[]{:S(2)}) %collective-permute-start.4) | collective-permute-done | bytes 151584 | tf_op jit(solution)/shard_map/ppermute | solution.py:381
  58.4 1.7 %collective-permute-done.5.refs_6_ = bf16[592,128]{1,0:T(8,128)(2,1)S(1)} collective-permute-done((bf16[592,128]{1,0:T(8,128)(2,1)}, bf16[592,128]{1,0:T(8,128)(2,1)S(1)}, u32[]{:S(2)}, u32[]{:S(2)}) %collective-permute-start.5) | collective-permute-done | bytes 151584 | tf_op jit(solution)/shard_map/ppermute | solution.py:381
  60.1 7.5 %collective-permute-done.6.refs_7_ = bf16[592,128]{1,0:T(8,128)(2,1)S(1)} collective-permute-done((bf16[592,128]{1,0:T(8,128)(2,1)}, bf16[592,128]{1,0:T(8,128)(2,1)S(1)}, u32[]{:S(2)}, u32[]{:S(2)}) %collective-permute-start.6) | collective-permute-done | bytes 151584 | tf_op jit(solution)/shard_map/ppermute | solution.py:381
  67.6 0.0 copy-done.10
  67.6 0.0 copy-start.8
  67.6 0.9 copy-done.8
  68.5 5.7 %shard_map.105 = (bf16[1136,128]{1,0:T(8,128)(2,1)S(1)}, bf16[1136,128]{1,0:T(8,128)(2,1)S(1)}, bf16[1136,128]{1,0:T(8,128)(2,1)S(1)}, bf16[1136,128]{1,0:T(8,128)(2,1)S(1)}) custom-call(s32[4]{0:T(128)S(1)} %pad_add_fusion.place, s32[768]{0:T(1024)S(1)} %reshape.19.doc, s32[128]{0:T(128)S(1)} %copy-done.10, bf16[592,128]{1,0:T(8,128)(2,1)S(1)} %copy-done.8, ...), custom_call_target="tpu_custom_call" | custom-call | tf_op jit(solution)/shard_map/pallas_call | solution.py:173
  74.3 3.1 %collective-permute-start.7 = (bf16[1136,128]{1,0:T(8,128)(2,1)S(1)}, bf16[1136,128]{1,0:T(8,128)(2,1)S(1)}, u32[]{:S(2)}, u32[]{:S(2)}) collective-permute-start(bf16[1136,128]{1,0:T(8,128)(2,1)S(1)} %get-tuple-element.25), channel_id=1, source_target_pairs={{0,128},{16,144},{32,160},{48,176},{64,192},{80,208},{96,224},{112... | collective-permute-start | bytes 872456 | tf_op jit(solution)/shard_map/ppermute | solution.py:383
  77.4 2.7 %collective-permute-start.8 = (bf16[1136,128]{1,0:T(8,128)(2,1)S(1)}, bf16[1136,128]{1,0:T(8,128)(2,1)S(1)}, u32[]{:S(2)}, u32[]{:S(2)}) collective-permute-start(bf16[1136,128]{1,0:T(8,128)(2,1)S(1)} %get-tuple-element.26), channel_id=1, source_target_pairs={{0,256},{16,272},{32,288},{48,304},{64,320},{80,336},{96,352},{112... | collective-permute-start | bytes 872456 | tf_op jit(solution)/shard_map/ppermute | solution.py:383
  80.1 3.8 %collective-permute-start.9 = (bf16[1136,128]{1,0:T(8,128)(2,1)S(1)}, bf16[1136,128]{1,0:T(8,128)(2,1)S(1)}, u32[]{:S(2)}, u32[]{:S(2)}) collective-permute-start(bf16[1136,128]{1,0:T(8,128)(2,1)S(1)} %get-tuple-element.27), channel_id=1, source_target_pairs={{0,384},{16,400},{32,416},{48,432},{64,448},{80,464},{96,480},{112... | collective-permute-start | bytes 872456 | tf_op jit(solution)/shard_map/ppermute | solution.py:383
  83.9 0.2 collective-permute-done.7.refs_1_
  84.1 4.3 %collective-permute-done.8.refs_2_ = bf16[1136,128]{1,0:T(8,128)(2,1)S(1)} collective-permute-done((bf16[1136,128]{1,0:T(8,128)(2,1)S(1)}, bf16[1136,128]{1,0:T(8,128)(2,1)S(1)}, u32[]{:S(2)}, u32[]{:S(2)}) %collective-permute-start.8) | collective-permute-done | bytes 290848 | tf_op jit(solution)/shard_map/ppermute | solution.py:383
  88.5 7.4 %collective-permute-done.9.refs_3_ = bf16[1136,128]{1,0:T(8,128)(2,1)S(1)} collective-permute-done((bf16[1136,128]{1,0:T(8,128)(2,1)S(1)}, bf16[1136,128]{1,0:T(8,128)(2,1)S(1)}, u32[]{:S(2)}, u32[]{:S(2)}) %collective-permute-start.9) | collective-permute-done | bytes 290848 | tf_op jit(solution)/shard_map/ppermute | solution.py:383
  95.9 2.1 %shard_map.106 = (bf16[1552,128]{1,0:T(8,128)(2,1)S(1)}, bf16[16,768]{1,0:T(8,128)(2,1)S(1)}) custom-call(s32[4]{0:T(128)S(1)} %pad_add_fusion.place, s32[768]{0:T(1024)S(1)} %reshape.19.doc, s32[128]{0:T(128)S(1)} %copy-done.10, bf16[1136,128]{1,0:T(8,128)(2,1)S(1)} %get-tuple-element.24.refs_0_, bf16[1136,128]{1,0:T(8,128)(2,1)S(1)} %collective-permute-done.7.refs_1_, ...), custom_call_target="tpu_custom_call" | custom-call | tf_op jit(solution)/shard_map/pallas_call | solution.py:229
  97.9 2.4 %collective-permute-start.10 = (bf16[1552,128]{1,0:T(8,128)(2,1)S(1)}, bf16[1552,128]{1,0:T(8,128)(2,1)S(1)}, u32[]{:S(2)}, u32[]{:S(2)}) collective-permute-start(bf16[1552,128]{1,0:T(8,128)(2,1)S(1)} %get-tuple-element.28.far_mine.mine), channel_id=1, source_target_pairs={{0,1},{1,0},{2,3},{3,2},{4,5},{5,4},{6,7},{7,6},{8,9},{9,8},{10,11... | collective-permute-start | bytes 1191944 | tf_op jit(solution)/shard_map/ppermute | solution.py:385
  100.3 0.0 all-to-all-done
  100.4 1.9 %collective-permute-start.11 = (bf16[1024,128]{1,0:T(8,128)(2,1)S(1)}, bf16[1024,128]{1,0:T(8,128)(2,1)S(1)}, u32[]{:S(2)}, u32[]{:S(2)}) collective-permute-start(bf16[1024,128]{1,0:T(8,128)(2,1)S(1)} %slice.4.near_mine), channel_id=1, source_target_pairs={{0,1},{1,0},{2,3},{3,2},{4,5},{5,4},{6,7},{7,6},{8,9},{9,8},{10,11... | collective-permute-start | bytes 786440 | tf_op jit(solution)/shard_map/ppermute | solution.py:389
  102.3 0.0 copy-done
  102.3 0.2 dynamic-slice_reduce_fusion.lens
  102.5 0.0 collective-permute-done.10.far_other.other
  102.5 1.7 %shard_map.109 = bf16[6,768]{1,0:T(8,128)(2,1)} custom-call(s32[4]{0:T(128)S(1)} %pad_add_fusion.place, s32[3]{0:T(128)S(1)} %dynamic-slice_reduce_fusion.lens, bf16[1552,128]{1,0:T(8,128)(2,1)S(1)} %get-tuple-element.28.far_mine.mine, bf16[1552,128]{1,0:T(8,128)(2,1)S(1)} %collective-permute-done.10.far_other.other, bf16[16,768]{1,0:T(8,128)(2,1)S(1)} %get-tuple-element.29.q_ref), custom_call_target="tpu_custom_call" | custom-call | tf_op jit(solution)/shard_map/pallas_call | solution.py:287
  104.2 0.0 collective-permute-done.11.near_other
  104.2 16.5 %shard_map.108 = bf16[1024,768]{1,0:T(8,128)(2,1)} custom-call(s32[4]{0:T(128)S(1)} %pad_add_fusion.place, s32[3]{0:T(128)S(1)} %dynamic-slice_reduce_fusion.lens, bf16[1552,128]{1,0:T(8,128)(2,1)S(1)} %get-tuple-element.28.far_mine.mine, bf16[1552,128]{1,0:T(8,128)(2,1)S(1)} %collective-permute-done.10.far_other.other, ...), custom_call_target="tpu_custom_call" | custom-call | tf_op jit(solution)/shard_map/pallas_call | solution.py:342
  (1 shorter events, 0.0 us)
Async XLA Ops:
  0.6 101.7 %copy-start = (s32[32,3]{0,1:T(4,128)S(1)}, s32[32,3]{0,1:T(4,128)}, u32[]{:S(2)}) copy-start(s32[32,3]{0,1:T(4,128)} %param.12) | copy-start | bytes 1156
  0.6 1.4 %copy-start.2 = (bf16[1,64,12288]{2,1,0:T(8,128)(2,1)S(1)}, bf16[1,64,12288]{2,1,0:T(8,128)(2,1)}, u32[]{:S(2)}) copy-start(bf16[1,64,12288]{2,1,0:T(8,128)(2,1)} %param.13) | copy-start | bytes 4718596
  2.1 0.9 copy-start.6
  3.7 1.3 %copy-start.1 = (bf16[16,64,896]{2,1,0:T(8,128)(2,1)}, bf16[16,64,896]{2,1,0:T(8,128)(2,1)S(1)}, u32[]{:S(2)}) copy-start(bf16[16,64,896]{2,1,0:T(8,128)(2,1)S(1)} %shard_map.107) | copy-start | bytes 5505028
  4.9 11.2 %copy-start.3 = (bf16[384,2048]{1,0:T(8,128)(2,1)S(1)}, bf16[384,2048]{1,0:T(8,128)(2,1)}, u32[]{:S(2)}) copy-start(bf16[384,2048]{1,0:T(8,128)(2,1)} %wkv_ref.1) | copy-start | bytes 4718596
  4.9 95.4 %all-to-all-start = ((bf16[16,64,896]{2,1,0:T(8,128)(2,1)}), bf16[16,64,896]{2,1,0:T(8,128)(2,1)S(1)}, u32[]{:S(2)}, u32[]{:S(2)}) async-start(bf16[16,64,896]{2,1,0:T(8,128)(2,1)} %copy-done.1), calls=%async_computation | async-start | bytes 3670016 | tf_op jit(solution)/shard_map/all_to_all | solution.py:377
  16.2 1.2 %copy-start.4 = (bf16[4,64,2048]{2,1,0:T(8,128)(2,1)S(1)}, bf16[4,64,2048]{2,1,0:T(8,128)(2,1)}, u32[]{:S(2)}) copy-start(bf16[4,64,2048]{2,1,0:T(8,128)(2,1)} %pages_ref.1) | copy-start | bytes 3145732
  17.4 1.1 copy-start.5
  18.4 0.9 copy-start.9
  19.4 30.3 %copy-start.11 = (s32[32,3,8]{0,2,1:T(8,128)S(1)}, s32[32,3,8]{0,2,1:T(8,128)}, u32[]{:S(2)}) copy-start(s32[32,3,8]{0,2,1:T(8,128)} %param.11) | copy-start | bytes 9220
  19.4 48.2 %copy-start.10 = (s32[128]{0:T(128)S(1)}, s32[128]{0:T(128)}, u32[]{:S(2)}) copy-start(s32[128]{0:T(128)} %home.3) | copy-start | bytes 1540
  21.4 0.7 copy-start.7
  22.0 19.2 %collective-permute-start = (bf16[592,128]{1,0:T(8,128)(2,1)S(1)}, bf16[592,128]{1,0:T(8,128)(2,1)S(1)}, u32[]{:S(2)}, u32[]{:S(2)}) collective-permute-start(bf16[592,128]{1,0:T(8,128)(2,1)S(1)} %get-tuple-element.17), channel_id=1, source_target_pairs={{0,16},{16,32},{32,48},{48,64},{64,80},{80,96},{96,112},{112,0},{1... | collective-permute-start | bytes 454664 | tf_op jit(solution)/shard_map/ppermute | solution.py:381
  25.2 20.2 %collective-permute-start.1 = (bf16[592,128]{1,0:T(8,128)(2,1)S(1)}, bf16[592,128]{1,0:T(8,128)(2,1)S(1)}, u32[]{:S(2)}, u32[]{:S(2)}) collective-permute-start(bf16[592,128]{1,0:T(8,128)(2,1)S(1)} %get-tuple-element.18), channel_id=1, source_target_pairs={{0,32},{16,48},{32,64},{48,80},{64,96},{80,112},{96,0},{112,16},{1... | collective-permute-start | bytes 454664 | tf_op jit(solution)/shard_map/ppermute | solution.py:381
  30.7 19.1 %collective-permute-start.2 = (bf16[592,128]{1,0:T(8,128)(2,1)}, bf16[592,128]{1,0:T(8,128)(2,1)S(1)}, u32[]{:S(2)}, u32[]{:S(2)}) collective-permute-start(bf16[592,128]{1,0:T(8,128)(2,1)} %get-tuple-element.19), channel_id=1, source_target_pairs={{0,48},{16,64},{32,80},{48,96},{64,112},{80,0},{96,16},{112,32},{1... | collective-permute-start | bytes 454664 | tf_op jit(solution)/shard_map/ppermute | solution.py:381
  33.2 16.6 %collective-permute-start.3 = (bf16[592,128]{1,0:T(8,128)(2,1)}, bf16[592,128]{1,0:T(8,128)(2,1)S(1)}, u32[]{:S(2)}, u32[]{:S(2)}) collective-permute-start(bf16[592,128]{1,0:T(8,128)(2,1)} %get-tuple-element.20), channel_id=1, source_target_pairs={{0,64},{16,80},{32,96},{48,112},{64,0},{80,16},{96,32},{112,48},{1... | collective-permute-start | bytes 454664 | tf_op jit(solution)/shard_map/ppermute | solution.py:381
  37.7 20.8 %collective-permute-start.4 = (bf16[592,128]{1,0:T(8,128)(2,1)}, bf16[592,128]{1,0:T(8,128)(2,1)S(1)}, u32[]{:S(2)}, u32[]{:S(2)}) collective-permute-start(bf16[592,128]{1,0:T(8,128)(2,1)} %get-tuple-element.21), channel_id=1, source_target_pairs={{0,80},{16,96},{32,112},{48,0},{64,16},{80,32},{96,48},{112,64},{1... | collective-permute-start | bytes 454664 | tf_op jit(solution)/shard_map/ppermute | solution.py:381
  41.3 18.8 %collective-permute-start.5 = (bf16[592,128]{1,0:T(8,128)(2,1)}, bf16[592,128]{1,0:T(8,128)(2,1)S(1)}, u32[]{:S(2)}, u32[]{:S(2)}) collective-permute-start(bf16[592,128]{1,0:T(8,128)(2,1)} %get-tuple-element.22), channel_id=1, source_target_pairs={{0,96},{16,112},{32,0},{48,16},{64,32},{80,48},{96,64},{112,80},{1... | collective-permute-start | bytes 454664 | tf_op jit(solution)/shard_map/ppermute | solution.py:381
  45.4 22.2 %collective-permute-start.6 = (bf16[592,128]{1,0:T(8,128)(2,1)}, bf16[592,128]{1,0:T(8,128)(2,1)S(1)}, u32[]{:S(2)}, u32[]{:S(2)}) collective-permute-start(bf16[592,128]{1,0:T(8,128)(2,1)} %get-tuple-element.23), channel_id=1, source_target_pairs={{0,112},{16,0},{32,16},{48,32},{64,48},{80,64},{96,80},{112,96},{1... | collective-permute-start | bytes 454664 | tf_op jit(solution)/shard_map/ppermute | solution.py:381
  67.6 0.9 copy-start.8
  74.3 9.9 %collective-permute-start.7 = (bf16[1136,128]{1,0:T(8,128)(2,1)S(1)}, bf16[1136,128]{1,0:T(8,128)(2,1)S(1)}, u32[]{:S(2)}, u32[]{:S(2)}) collective-permute-start(bf16[1136,128]{1,0:T(8,128)(2,1)S(1)} %get-tuple-element.25), channel_id=1, source_target_pairs={{0,128},{16,144},{32,160},{48,176},{64,192},{80,208},{96,224},{112... | collective-permute-start | bytes 872456 | tf_op jit(solution)/shard_map/ppermute | solution.py:383
  77.4 11.1 %collective-permute-start.8 = (bf16[1136,128]{1,0:T(8,128)(2,1)S(1)}, bf16[1136,128]{1,0:T(8,128)(2,1)S(1)}, u32[]{:S(2)}, u32[]{:S(2)}) collective-permute-start(bf16[1136,128]{1,0:T(8,128)(2,1)S(1)} %get-tuple-element.26), channel_id=1, source_target_pairs={{0,256},{16,272},{32,288},{48,304},{64,320},{80,336},{96,352},{112... | collective-permute-start | bytes 872456 | tf_op jit(solution)/shard_map/ppermute | solution.py:383
  80.1 15.7 %collective-permute-start.9 = (bf16[1136,128]{1,0:T(8,128)(2,1)S(1)}, bf16[1136,128]{1,0:T(8,128)(2,1)S(1)}, u32[]{:S(2)}, u32[]{:S(2)}) collective-permute-start(bf16[1136,128]{1,0:T(8,128)(2,1)S(1)} %get-tuple-element.27), channel_id=1, source_target_pairs={{0,384},{16,400},{32,416},{48,432},{64,448},{80,464},{96,480},{112... | collective-permute-start | bytes 872456 | tf_op jit(solution)/shard_map/ppermute | solution.py:383
  97.9 4.6 %collective-permute-start.10 = (bf16[1552,128]{1,0:T(8,128)(2,1)S(1)}, bf16[1552,128]{1,0:T(8,128)(2,1)S(1)}, u32[]{:S(2)}, u32[]{:S(2)}) collective-permute-start(bf16[1552,128]{1,0:T(8,128)(2,1)S(1)} %get-tuple-element.28.far_mine.mine), channel_id=1, source_target_pairs={{0,1},{1,0},{2,3},{3,2},{4,5},{5,4},{6,7},{7,6},{8,9},{9,8},{10,11... | collective-permute-start | bytes 1191944 | tf_op jit(solution)/shard_map/ppermute | solution.py:385
  100.4 3.8 %collective-permute-start.11 = (bf16[1024,128]{1,0:T(8,128)(2,1)S(1)}, bf16[1024,128]{1,0:T(8,128)(2,1)S(1)}, u32[]{:S(2)}, u32[]{:S(2)}) collective-permute-start(bf16[1024,128]{1,0:T(8,128)(2,1)S(1)} %slice.4.near_mine), channel_id=1, source_target_pairs={{0,1},{1,0},{2,3},{3,2},{4,5},{5,4},{6,7},{7,6},{8,9},{9,8},{10,11... | collective-permute-start | bytes 786440 | tf_op jit(solution)/shard_map/ppermute | solution.py:389
